TPU v7x, 32 devices: a whole 2x2x4 slice. The times are simulated.
32 devices in a mesh: member: 8 (over y, x, core), lat: 4 (over z).
Axes of the slice: x: 2, y: 2, z: 4, core: 2. Of those that a mesh axis runs over, the one named last changes fastest.
Arguments:
- noisy_latents: bfloat16 [8, 64, 32, 768], P('member', 'lat'), may hold values from -6 to 6
- frames: bfloat16 [8, 64, 32, 768], P('member', 'lat'), may hold values from -6 to 6
- encoder_members: int32 [2], replicated, may hold values from 0 to 7, as said below
- window_shift: int32 [1], replicated, may hold values from 1 to 7
- encoder_in: bfloat16 [768, 768], replicated, may hold values from -0.21875 to 0.21875
- encoder_out: bfloat16 [768, 768], replicated, may hold values from -0.21875 to 0.21875
- joint_weight: bfloat16 [2304, 768], replicated, may hold values from -0.125 to 0.125
- query_weight: bfloat16 [768, 768], replicated, may hold values from -0.21875 to 0.21875
- keyvalue_weight: bfloat16 [768, 1536], replicated, may hold values from -0.21875 to 0.21875
- output_weight: bfloat16 [768, 768], replicated, may hold values from -0.21875 to 0.21875
- position_bias: float32 [12, 225], replicated, may hold values from -250 to 250
- expand_weight: bfloat16 [3072, 768], P('member'), may hold values from -0.21875 to 0.21875
- reduce_weight: bfloat16 [3072, 768], P('member'), may hold values from -0.109375 to 0.109375
Outputs:
- block_out: bfloat16 [8, 64, 32, 768], P('member', 'lat')
Inputs may be any that keep to these rules, and one draw needn't show every extreme that they name: `encoder_members`: two different members, one of which is the last member, 7, in either position.
All inputs are finite; a program needn't handle non-finite values.
Results may differ from a plain program's by a relative error of at most 0.013.
Values may be sent and summed in bfloat16 or wider, within the bound.
A program may use at most 128 MiB of HBM per device.

v0:
```python
import jax
import jax.numpy as jnp
import numpy as np
from jax import lax
from jax.sharding import PartitionSpec as P

HD = 64
WIN = 8


epsilon = 1e-06


def broadcast(array, axis, root):
    mine = lax.axis_index(axis) == root
    return lax.psum(jnp.where(mine, array, jnp.zeros_like(array)), axis)


def padded(cells, sides, width):
    for axis, dim in sides:
        count = lax.axis_size(axis)
        ends = count - 1
        head = lax.slice_in_dim(cells, 0, width, axis=dim)
        tail = lax.slice_in_dim(cells, cells.shape[dim] - width, cells.shape[dim], axis=dim)
        cells = jnp.concatenate(
            [
                lax.ppermute(tail, axis, [(i, (i + 1) % count) for i in range(ends)]),
                cells,
                lax.ppermute(head, axis, [((i + 1) % count, i) for i in range(ends)]),
            ],
            axis=dim,
        )
    return cells


def offset_table(win):
    position = np.arange(win * win)
    row_pos = position // win
    col_pos = position % win
    row_diff = row_pos[None, :] - row_pos[:, None] + win - 1
    col_diff = col_pos[None, :] - col_pos[:, None] + win - 1
    return (row_diff * (2 * win - 1) + col_diff).astype(np.int32)


def rms_norm(values):
    scale = lax.rsqrt(jnp.mean(values * values, axis=-1, keepdims=True) + epsilon)
    return (values * scale).astype(jnp.bfloat16)


def encode(frame, encoder_in, encoder_out):
    hidden = jax.nn.gelu(jnp.dot(frame, encoder_in, preferred_element_type=jnp.float32)).astype(
        jnp.bfloat16
    )
    return jnp.dot(hidden, encoder_out, preferred_element_type=jnp.float32).astype(jnp.bfloat16)


def window_attention(query, key_rows, value_rows, valid, position_bias, shift):
    nrows, ncols, width = query.shape
    heads = width // HD
    row_groups, col_groups = (nrows // WIN, ncols // WIN)

    def arrange(block):
        block = jnp.roll(block, shift, axis=1)
        block = block.reshape(row_groups, WIN, col_groups, WIN, heads, HD)
        return block.transpose(0, 2, 4, 1, 3, 5).reshape(
            row_groups * col_groups, heads, WIN * WIN, HD
        )

    query_win = arrange(query)
    key_win = arrange(key_rows)
    value_win = arrange(value_rows)
    keep = jnp.broadcast_to(
        valid.reshape(row_groups, 1, WIN, 1), (row_groups, col_groups, WIN, WIN)
    )
    keep = keep.reshape(row_groups * col_groups, 1, 1, WIN * WIN)
    bias = position_bias[:, offset_table(WIN)]
    scores = jnp.einsum("whqd,whkd->whqk", query_win, key_win, preferred_element_type=jnp.float32)
    scores = scores * HD ** (-0.5) + bias[None]
    scores = jnp.where(keep, scores, -1e30)
    highest = jnp.max(scores, axis=-1, keepdims=True)
    weights = jnp.exp(scores - highest)
    probs = (weights / jnp.sum(weights, axis=-1, keepdims=True)).astype(jnp.bfloat16)
    mixed = jnp.einsum(
        "whqk,whkd->whqd", probs, value_win, preferred_element_type=jnp.float32
    ).astype(jnp.bfloat16)
    mixed = mixed.reshape(row_groups, col_groups, heads, WIN, WIN, HD).transpose(0, 3, 1, 4, 2, 5)
    return jnp.roll(mixed.reshape(nrows, ncols, width), -shift, axis=1)


def per_device(
    noisy_latents,
    frames,
    encoder_members,
    window_shift,
    encoder_in,
    encoder_out,
    joint_weight,
    query_weight,
    keyvalue_weight,
    output_weight,
    position_bias,
    expand_weight,
    reduce_weight,
):
    width = noisy_latents.shape[-1]
    noisy_band = noisy_latents[0]
    frame_band = frames[0]
    nrows = noisy_band.shape[0]
    margin = WIN // 2
    shift = window_shift[0]
    noisy_term = jnp.dot(noisy_band, joint_weight[:width], preferred_element_type=jnp.float32)
    conditions = []
    for member_slot in range(2):
        arrived = broadcast(frame_band, "member", encoder_members[member_slot])
        conditions.append(encode(arrived, encoder_in, encoder_out))
    joined = noisy_term + jnp.dot(
        conditions[0], joint_weight[width : 2 * width], preferred_element_type=jnp.float32
    )
    joined = joined + jnp.dot(
        conditions[1], joint_weight[2 * width :], preferred_element_type=jnp.float32
    )
    stream = joined.astype(jnp.bfloat16)
    normed = rms_norm(stream.astype(jnp.float32))
    query = jnp.dot(normed, query_weight, preferred_element_type=jnp.float32).astype(jnp.bfloat16)
    keyvalue = jnp.dot(normed, keyvalue_weight, preferred_element_type=jnp.float32).astype(
        jnp.bfloat16
    )
    keyvalue_wide = padded(keyvalue, (("lat", 0),), margin)
    band_index = lax.axis_index("lat")
    band_count = lax.axis_size("lat")
    extended = jnp.arange(nrows + 2 * margin)
    valid = jnp.logical_and(
        jnp.logical_or(band_index > 0, extended >= margin),
        jnp.logical_or(band_index < band_count - 1, extended < nrows + margin),
    )
    query_wide = jnp.pad(query, ((margin, margin), (0, 0), (0, 0)))
    mixed = window_attention(
        query_wide,
        keyvalue_wide[..., :width],
        keyvalue_wide[..., width:],
        valid,
        position_bias,
        shift,
    )[margin : margin + nrows]
    attended = (
        stream.astype(jnp.float32)
        + jnp.dot(mixed, output_weight, preferred_element_type=jnp.float32)
    ).astype(jnp.bfloat16)
    second_normed = rms_norm(attended.astype(jnp.float32)).reshape(-1, width)
    contract_rows = (((1,), (1,)), ((), ()))
    hidden = jax.nn.gelu(
        lax.dot_general(
            second_normed,
            lax.all_gather(expand_weight, "member", axis=0, tiled=True),
            contract_rows,
            preferred_element_type=jnp.float32,
        )
    ).astype(jnp.bfloat16)
    update = jnp.dot(
        hidden,
        lax.all_gather(reduce_weight, "member", axis=0, tiled=True),
        preferred_element_type=jnp.float32,
    )
    result = (attended.reshape(-1, width).astype(jnp.float32) + update).astype(jnp.bfloat16)
    return result.reshape(noisy_latents.shape)


def solution(mesh):
    return jax.shard_map(
        per_device,
        mesh=mesh,
        in_specs=(
            P("member", "lat", None, None),
            P("member", "lat", None, None),
            P(),
            P(),
            P(),
            P(),
            P(),
            P(),
            P(),
            P(),
            P(),
            P("member", None),
            P("member", None),
        ),
        out_specs=P("member", "lat", None, None),
        check_vma=False,
    )
```

profile of v0, /device:TPU:0, one launch (start us, length us, event | category | flops | bytes accessed | tf_op | source)
XLA Modules:
  0.0 171.8 jit_solution(3867680426439285352)
XLA Ops:
  6.5 1.4 fusion.92
  9.1 2.4 %select_bitcast_fusion = (bf16[16,32,768]{2,1,0:T(8,128)(2,1)}, bf16[16,32,768]{2,1,0:T(8,128)(2,1)}) fusion(bf16[1,16,32,768]{3,2,1,0:T(8,128)(2,1)} %param.18, pred[]{:T(512)S(6)} %eq.9, pred[]{:T(512)S(6)} %eq.8), kind=kLoop, calls=%fused_computation.87 | loop fusion | flops 786432 | bytes 2359298 | tf_op jit(solution)/shard_map/jit(_where)/select_n | solution.py:16
  14.1 14.1 %gather_fusion = f32[4096,12]{1,0:T(8,128)} fusion(f32[12,225]{0,1:T(8,128)S(1)} %copy.22, s32[4096]{0:T(1024)S(1)} %broadcast_clamp_fusion), kind=kCustom, calls=%fused_computation | custom fusion | bytes 409600 | tf_op jit(solution)/shard_map/gather | solution.py:76
  28.2 2.8 %copy.23 = f32[64,64,12]{0,1,2:T(8,128)S(1)} copy(f32[64,64,12]{2,1,0:T(8,128)} %bitcast.86) | data formatting | bytes 393216 | tf_op jit(solution)/shard_map/gather | solution.py:76
  31.0 3.2 %fusion.57 = f32[16,32,768]{2,1,0:T(8,128)} fusion(bf16[2304,768]{1,0:T(8,128)(2,1)} %param.23, bf16[1,16,32,768]{3,2,1,0:T(8,128)(2,1)S(1)} %copy-done.10), kind=kOutput, calls=%fused_computation.81 | convolution fusion | flops 603979776 | bytes 3538944 | tf_op jit(solution)/shard_map/dot_general | solution.py:111
  34.2 39.3 %all-reduce.4.cloned.1.call-done = (bf16[16,32,768]{2,1,0:T(8,128)(2,1)}, bf16[16,32,768]{2,1,0:T(8,128)(2,1)}) async-done(((bf16[16,32,768]{2,1,0:T(8,128)(2,1)}, bf16[16,32,768]{2,1,0:T(8,128)(2,1)}), (bf16[16,32,768]{2,1,0:T(8,128)(2,1)}, bf16[16,32,768]{2,1,0:T(8,128)(2,1)})) %all-reduce.4.cloned.1.call-update) | async-done | bytes 1572880 | tf_op jit(solution)/shard_map/psum | solution.py:16
  73.5 2.5 %fusion.27 = bf16[16,32,768]{2,1,0:T(8,128)(2,1)S(1)} fusion(bf16[16,32,768]{2,1,0:T(8,128)(2,1)} %get-tuple-element.6, bf16[768,768]{1,0:T(8,128)(2,1)} %param.21), kind=kOutput, calls=%fused_computation.47 | convolution fusion | flops 607518720 | bytes 2752512 | tf_op jit(solution)/shard_map/dot_general | solution.py:51
  76.0 4.3 %fusion.51 = f32[16,32,768]{2,1,0:T(8,128)} fusion(bf16[2304,768]{1,0:T(8,128)(2,1)} %param.23, bf16[16,32,768]{2,1,0:T(8,128)(2,1)S(1)} %fusion.27, bf16[768,768]{1,0:T(8,128)(2,1)} %param.22), kind=kOutput, calls=%fused_computation.75 | convolution fusion | flops 1208352768 | bytes 4718592 | tf_op jit(solution)/shard_map/dot_general | solution.py:116
  80.3 3.6 %convolution_convert_fusion.2 = bf16[16,32,768]{2,1,0:T(8,128)(2,1)S(1)} fusion(bf16[768,768]{1,0:T(8,128)(2,1)} %param.22, bf16[16,32,768]{2,1,0:T(8,128)(2,1)} %get-tuple-element.7, bf16[768,768]{1,0:T(8,128)(2,1)} %param.21), kind=kOutput, calls=%fused_computation.66 | convolution fusion | flops 1211891712 | bytes 3932160 | tf_op jit(solution)/shard_map/dot_general | solution.py:54
  84.0 3.1 %fusion.36 = (f32[16,32]{1,0:T(8,128)S(1)}, bf16[16,32,768]{2,1,0:T(8,128)(2,1)S(1)}) fusion(bf16[16,32,768]{2,1,0:T(8,128)(2,1)S(1)} %convolution_convert_fusion.2, bf16[2304,768]{1,0:T(8,128)(2,1)} %param.23, f32[16,32,768]{2,1,0:T(8,128)} %fusion.57, f32[16,32,768]{2,1,0:T(8,128)} %fusion.51), kind=kOutput, calls=%fused_computation.56 | convolution fusion | flops 606338560 | bytes 5900288 | tf_op jit(solution)/shard_map/dot_general | solution.py:119
  87.1 1.4 convolution_convert_fusion
  88.6 0.9 fusion.91
  89.5 4.4 %collective-permute-start = (bf16[4,32,1536]{2,1,0:T(8,128)(2,1)}, bf16[4,32,1536]{2,1,0:T(8,128)(2,1)}, u32[]{:S(2)}, u32[]{:S(2)}) collective-permute-start(bf16[4,32,1536]{2,1,0:T(8,128)(2,1)} %get-tuple-element.10), channel_id=1, source_target_pairs={{0,1},{1,2},{2,3},{4,5},{5,6},{6,7},{8,9},{9,10},{10,11},{12,13},{... | collective-permute-start | bytes 1179656 | tf_op jit(solution)/shard_map/ppermute | solution.py:27
  93.9 1.3 collective-permute-start.1
  96.2 1.9 %fusion.47 = bf16[24,32,768]{2,1,0:T(8,128)(2,1)} fusion(s32[]{:T(128)S(6)} %select_n.52, bf16[24,32,768]{2,1,0:T(8,128)(2,1)S(1)} %pad.4), kind=kLoop, calls=%fused_computation.71 | loop fusion | flops 2359296 | bytes 2359300 | tf_op jit(solution)/shard_map/jit(_roll_dynamic)/concatenate | solution.py:63
  98.1 3.4 %reshape.74 = bf16[3,8,4,8,12,64]{5,4,3,2,1,0:T(8,128)(2,1)S(1)} reshape(bf16[24,32,768]{2,1,0:T(8,128)(2,1)} %fusion.47) | data formatting | bytes 2359296 | tf_op jit(solution)/shard_map/reshape | solution.py:64
  101.5 2.0 %copy.20 = bf16[3,4,12,8,8,64]{5,4,3,2,1,0:T(8,128)(2,1)} copy(bf16[3,4,12,8,8,64]{5,2,4,1,3,0:T(8,128)(2,1)S(1)} %bitcast.82) | data formatting | bytes 2359296 | tf_op jit(solution)/shard_map/transpose | solution.py:65
  103.6 2.1 %collective-permute-done.1 = bf16[4,32,1536]{2,1,0:T(8,128)(2,1)} collective-permute-done((bf16[4,32,1536]{2,1,0:T(8,128)(2,1)}, bf16[4,32,1536]{2,1,0:T(8,128)(2,1)}, u32[]{:S(2)}, u32[]{:S(2)}) %collective-permute-start.1) | collective-permute-done | bytes 393248 | tf_op jit(solution)/shard_map/ppermute | solution.py:29
  105.7 1.4 pad_maximum_fusion
  107.4 3.4 %fusion.45 = (bf16[24,32,768]{2,1,0:T(8,128)(2,1)}, bf16[24,32,768]{2,1,0:T(8,128)(2,1)}) fusion(s32[]{:T(128)S(6)} %select_n.52, bf16[24,32,768]{2,1,0:T(8,128)(2,1)S(1)} %get-tuple-element.9, bf16[24,32,768]{2,1,0:T(8,128)(2,1)S(1)} %get-tuple-element.8), kind=kLoop, calls=%fused_computation.69 | loop fusion | flops 4718592 | bytes 4718596 | tf_op jit(solution)/shard_map/jit(_roll_dynamic)/concatenate | solution.py:63
  110.8 3.4 %reshape.76 = bf16[3,8,4,8,12,64]{5,4,3,2,1,0:T(8,128)(2,1)S(1)} reshape(bf16[24,32,768]{2,1,0:T(8,128)(2,1)} %get-tuple-element.23) | data formatting | bytes 2359296 | tf_op jit(solution)/shard_map/reshape | solution.py:64
  114.2 2.1 %copy.21 = bf16[3,4,12,8,8,64]{5,4,3,2,1,0:T(8,128)(2,1)} copy(bf16[3,4,12,8,8,64]{5,2,4,1,3,0:T(8,128)(2,1)S(1)} %bitcast.83) | data formatting | bytes 2359296 | tf_op jit(solution)/shard_map/transpose | solution.py:65
  116.2 3.4 %reshape.78 = bf16[3,8,4,8,12,64]{5,4,3,2,1,0:T(8,128)(2,1)S(1)} reshape(bf16[24,32,768]{2,1,0:T(8,128)(2,1)} %get-tuple-element.22) | data formatting | bytes 2359296 | tf_op jit(solution)/shard_map/reshape | solution.py:64
  119.6 2.0 %copy.24 = bf16[3,4,12,8,8,64]{5,4,3,2,1,0:T(8,128)(2,1)} copy(bf16[3,4,12,8,8,64]{5,2,4,1,3,0:T(8,128)(2,1)S(1)} %bitcast.84) | data formatting | bytes 2359296 | tf_op jit(solution)/shard_map/transpose | solution.py:65
  121.7 7.3 %fusion.93 = (f32[12,12,64]{2,1,0:T(8,128)S(1)}, f32[12,12,64,64]{2,3,1,0:T(8,128)}) fusion(f32[12,64,64]{1,2,0:T(8,128)S(1)} %bitcast.92, pred[12,64]{1,0:T(8,128)(4,1)S(1)} %broadcast_in_dim.28, bf16[12,12,64,64]{3,2,1,0:T(8,128)(2,1)} %bitcast.87, bf16[12,12,64,64]{3,2,1,0:T(8,128)(2,1)} %bitcast.88), kind=kOutput, calls=%fused_computation.117 | convolution fusion | flops 78446656 | bytes 4952832 | tf_op jit(solution)/shard_map/sub | solution.py:81
  129.0 3.3 %fusion.19 = bf16[12,12,64,64]{3,2,1,0:T(8,128)(2,1)S(1)} fusion(bf16[12,12,64,64]{3,2,1,0:T(8,128)(2,1)S(1)} %bitcast.89, f32[12,12,64,64]{2,3,1,0:T(8,128)} %get-tuple-element.19, f32[12,12,64]{2,1,0:T(8,128)S(1)} %get-tuple-element.18), kind=kOutput, calls=%fused_computation.39 | convolution fusion | flops 77266944 | bytes 4755456 | tf_op jit(solution)/shard_map/whqk,whkd->whqd/dot_general | solution.py:83
  132.3 2.8 %copy.29 = bf16[3,4,12,8,8,64]{5,2,4,1,3,0:T(8,128)(2,1)S(1)} copy(bf16[3,4,12,8,8,64]{5,4,3,2,1,0:T(8,128)(2,1)S(1)} %bitcast.90) | data formatting | bytes 2359296 | tf_op jit(solution)/shard_map/reshape | solution.py:86
  135.1 3.0 %reshape.81 = bf16[24,32,768]{2,1,0:T(8,128)(2,1)} reshape(bf16[3,8,4,8,12,64]{5,4,3,2,1,0:T(8,128)(2,1)S(1)} %bitcast.85) | data formatting | bytes 2359296 | tf_op jit(solution)/shard_map/reshape | solution.py:87
  138.1 3.2 %multiply_reduce_fusion = (f32[16,32]{1,0:T(8,128)S(1)}, f32[16,32,768]{2,1,0:T(8,128)S(1)}) fusion(bf16[768,768]{1,0:T(8,128)(2,1)} %param.26, s32[]{:T(128)S(6)} %select_n.58, bf16[24,32,768]{2,1,0:T(8,128)(2,1)} %reshape.81, bf16[16,32,768]{2,1,0:T(8,128)(2,1)} %copy-done.6), kind=kOutput, calls=%fused_computation.62 | convolution fusion | flops 608697856 | bytes 4720644 | tf_op jit(solution)/shard_map/dot_general | solution.py:147
  141.4 1.1 copy-done.5
  142.7 12.2 %all-gather.5.cloned.1.call-done = bf16[3072,768]{1,0:T(8,128)(2,1)} async-done(((bf16[384,768]{1,0:T(8,128)(2,1)}), bf16[3072,768]{1,0:T(8,128)(2,1)}) %all-gather.5.cloned.1.call-update) | async-done | bytes 4718608 | tf_op jit(solution)/shard_map/all_gather | solution.py:161
  154.9 10.4 %fusion.39 = bf16[512,768]{1,0:T(8,128)(2,1)} fusion(f32[16,32,768]{2,1,0:T(8,128)} %copy-done.5, bf16[3072,768]{1,0:T(8,128)(2,1)} %all-gather.5.cloned.1.call-done, bf16[512,768]{1,0:T(8,128)(2,1)S(1)} %bitcast.91, bf16[3072,768]{1,0:T(8,128)(2,1)} %all-gather.3.cloned.1.call-done), kind=kOutput, calls=%fused_computation.60 | convolution fusion | flops 4846780416 | bytes 12582912 | tf_op jit(solution)/shard_map/dot_general | solution.py:159
  (40 shorter events, 3.3 us)
Async XLA Ops:
  6.5 80.6 %copy-start = (bf16[768,1536]{1,0:T(8,128)(2,1)S(1)}, bf16[768,1536]{1,0:T(8,128)(2,1)}, u32[]{:S(2)}) copy-start(bf16[768,1536]{1,0:T(8,128)(2,1)} %param.25) | copy-start | bytes 7077892
  6.5 67.0 %all-reduce.4.cloned.1.call-start = ((), (), s32[]{:S(2)}) async-start(), calls=%async_computation.2 | async-start | bytes 3145728 | tf_op jit(solution)/shard_map/psum | solution.py:16
  11.5 2.4 %copy-start.7 = (f32[12,225]{1,0:T(8,128)S(1)}, f32[12,225]{1,0:T(8,128)}, u32[]{:S(2)}) copy-start(f32[12,225]{1,0:T(8,128)} %param.27) | copy-start | bytes 32404
  11.5 2.5 %copy-start.8 = (s32[4096]{0:T(1024)S(1)}, s32[4096]{0:T(1024)}, u32[]{:S(2)}) copy-start(s32[4096]{0:T(1024)} %constant.83) | copy-start | bytes 49156
  11.6 131.1 %all-gather.3.cloned.1.call-start = ((), (), s32[]{:S(2)}) async-start(), calls=%async_computation | async-start | bytes 5308416 | tf_op jit(solution)/shard_map/all_gather | solution.py:154
  12.3 142.5 %all-gather.5.cloned.1.call-start = ((), (), s32[]{:S(2)}) async-start(), calls=%async_computation.1 | async-start | bytes 5308416 | tf_op jit(solution)/shard_map/all_gather | solution.py:161
  28.2 2.8 %copy-start.10 = (bf16[1,16,32,768]{3,2,1,0:T(8,128)(2,1)S(1)}, bf16[1,16,32,768]{3,2,1,0:T(8,128)(2,1)}, u32[]{:S(2)}) copy-start(bf16[1,16,32,768]{3,2,1,0:T(8,128)(2,1)} %param.17) | copy-start | bytes 2359300
  87.1 8.1 %copy-start.6 = (bf16[16,32,768]{2,1,0:T(8,128)(2,1)}, bf16[16,32,768]{2,1,0:T(8,128)(2,1)S(1)}, u32[]{:S(2)}) copy-start(bf16[16,32,768]{2,1,0:T(8,128)(2,1)S(1)} %get-tuple-element.17) | copy-start | bytes 2359300
  88.6 7.5 %copy-start.2 = (bf16[16,32,1536]{2,1,0:T(8,128)(2,1)}, bf16[16,32,1536]{2,1,0:T(8,128)(2,1)S(1)}, u32[]{:S(2)}) copy-start(bf16[16,32,1536]{2,1,0:T(8,128)(2,1)S(1)} %convolution_convert_fusion) | copy-start | bytes 4718596
  88.6 6.6 %copy-start.9 = (bf16[768,768]{1,0:T(8,128)(2,1)S(1)}, bf16[768,768]{1,0:T(8,128)(2,1)}, u32[]{:S(2)}) copy-start(bf16[768,768]{1,0:T(8,128)(2,1)} %param.24) | copy-start | bytes 3538948
  89.5 14.0 %collective-permute-start = (bf16[4,32,1536]{2,1,0:T(8,128)(2,1)}, bf16[4,32,1536]{2,1,0:T(8,128)(2,1)}, u32[]{:S(2)}, u32[]{:S(2)}) collective-permute-start(bf16[4,32,1536]{2,1,0:T(8,128)(2,1)} %get-tuple-element.10), channel_id=1, source_target_pairs={{0,1},{1,2},{2,3},{4,5},{5,6},{6,7},{8,9},{9,10},{10,11},{12,13},{... | collective-permute-start | bytes 1179656 | tf_op jit(solution)/shard_map/ppermute | solution.py:27
  93.9 11.7 %collective-permute-start.1 = (bf16[4,32,1536]{2,1,0:T(8,128)(2,1)}, bf16[4,32,1536]{2,1,0:T(8,128)(2,1)}, u32[]{:S(2)}, u32[]{:S(2)}) collective-permute-start(bf16[4,32,1536]{2,1,0:T(8,128)(2,1)} %get-tuple-element.11), channel_id=1, source_target_pairs={{1,0},{2,1},{3,2},{5,4},{6,5},{7,6},{9,8},{10,9},{11,10},{13,12},{... | collective-permute-start | bytes 1179656 | tf_op jit(solution)/shard_map/ppermute | solution.py:29
  101.5 4.1 %copy-start.3 = (bf16[16,32,1536]{2,1,0:T(8,128)(2,1)S(1)}, bf16[16,32,1536]{2,1,0:T(8,128)(2,1)}, u32[]{:S(2)}) copy-start(bf16[16,32,1536]{2,1,0:T(8,128)(2,1)} %copy-done.2) | copy-start | bytes 4718596
  121.7 7.3 %copy-start.4 = (bf16[3,4,12,8,8,64]{5,4,3,2,1,0:T(8,128)(2,1)S(1)}, bf16[3,4,12,8,8,64]{5,4,3,2,1,0:T(8,128)(2,1)}, u32[]{:S(2)}) copy-start(bf16[3,4,12,8,8,64]{5,4,3,2,1,0:T(8,128)(2,1)} %copy.24) | copy-start | bytes 3538948
  141.4 1.1 copy-start.5
  154.9 10.4 %copy-start.1 = (bf16[768,1536]{1,0:T(8,128)(2,1)S(1)}, bf16[768,1536]{1,0:T(8,128)(2,1)}, u32[]{:S(2)}) copy-start(bf16[768,1536]{1,0:T(8,128)(2,1)} %param.25) | copy-start | bytes 7077892
Sparse Core Ops, SparseCore 0:
  11.7 61.7 all-reduce.3
  75.6 38.2 all-gather.2
  115.9 38.9 all-gather.4
where the time goes:
time: 172 us
  waiting for transfers between devices  55 us (32%)
  matrix products  43.3 us (25%)
  local copies, waits for them, and re-layouts  43.2 us (25%)
  between operations  15.2 us (9%)
  other arithmetic  9.32 us (5%)
  starting transfers between devices  5.74 us (3%)
    psum x1, waiting for transfers between devices, broadcast(): return lax.psum(jnp.where(mine, array, jnp.zeros_like(array)), axis)  39.3 us
    gather x2, local copies, waits for them, and re-layouts, window_attention(): bias = position_bias[:, offset_table(WIN)]  16.9 us
    all_gather x1, waiting for transfers between devices, per_device(): lax.all_gather(reduce_weight, 'member', axis=0, tiled=True)  12.2 us
    dot_general x1, matrix products, per_device(): jnp.dot(hidden, lax.all_gather(reduce_weight, 'member', axis=0, tiled=Tru...  10.4 us
    reshape x3, local copies, waits for them, and re-layouts, arrange(): block = block.reshape(row_groups, WIN, col_groups, WIN, heads, HD)  10.2 us
    sub x1, matrix products, window_attention(): weights = jnp.exp(scores - highest)  7.33 us
    transpose x3, local copies, waits for them, and re-layouts, arrange(): block.transpose(0, 2, 4, 1, 3, 5)  6.12 us
    concatenate x2, other arithmetic, arrange(): block = jnp.roll(block, shift, axis=1)  5.35 us
  transfers between devices with their start and end apart: 5, of which 3 were waited for; matrix products, arithmetic and copies ran while one was open for 47% of the time, Pallas kernels for 0%

commit v1 on v0

--- a/solution.py
+++ b/solution.py
@@ -2,6 +2,8 @@
 import jax.numpy as jnp
 import numpy as np
 from jax import lax
+from jax.experimental import pallas as pl
+from jax.experimental.pallas import tpu as pltpu
 from jax.sharding import PartitionSpec as P
 
 HD = 64
@@ -165,9 +167,521 @@
     return result.reshape(noisy_latents.shape)
 
 
+BF = jnp.bfloat16
+F32 = jnp.float32
+MESH = pl.DeviceIdType.MESH
+
+
+def fused_kernel(
+    enc_ref,
+    shift_ref,
+    noisy_hbm,
+    frames_hbm,
+    ein_hbm,
+    eout_hbm,
+    joint_hbm,
+    qw_hbm,
+    kvw_hbm,
+    ow_hbm,
+    table_ref,
+    exp_hbm,
+    red_hbm,
+    out_ref,
+    noisy,
+    ein,
+    eout,
+    joint,
+    qw,
+    kvw,
+    ow,
+    wexp,
+    wred,
+    arrived,
+    term,
+    total,
+    stream,
+    nx,
+    q,
+    kv,
+    mixed,
+    bias,
+    padded_table,
+    spread,
+    local_sem,
+    f_send,
+    f_recv,
+    t_send,
+    t_recv,
+    w_send,
+    w_recv,
+    h_send,
+    h_recv,
+):
+    member = lax.axis_index("member")
+    lat = lax.axis_index("lat")
+    lats = lax.axis_size("lat")
+    tokens, width = noisy.shape
+    piece = tokens // 8
+    group = tokens // 4
+    part = wexp.shape[1]
+    cols = group // (WIN // 2)
+    heads = table_ref.shape[0]
+    y, x, c = member // 4, (member // 2) % 2, member % 2
+
+    def flip(d):
+        return ((y + d // 4) % 2) * 4 + ((x + (d // 2) % 2) % 2) * 2 + (c + d % 2) % 2
+
+    local = {}
+    todo = [
+        ("noisy", noisy_hbm, noisy),
+        ("joint", joint_hbm, joint),
+        ("ein", ein_hbm, ein),
+        ("eout", eout_hbm, eout),
+        ("qw", qw_hbm, qw),
+        ("kvw", kvw_hbm, kvw),
+        ("ow", ow_hbm, ow),
+        ("exp", exp_hbm, wexp.at[member]),
+        ("red", red_hbm, wred.at[member]),
+        ("frame", frames_hbm.at[pl.ds(member * piece, piece)], arrived.at[member]),
+    ]
+    for i, (name, source, target) in enumerate(todo):
+        local[name] = pltpu.make_async_copy(source, target, local_sem.at[i])
+
+    def frame_copy(d, incoming=False):
+        other = flip(d)
+        slot = other if incoming else member
+        return pltpu.make_async_remote_copy(
+            src_ref=frames_hbm.at[pl.ds(other * piece, piece)],
+            dst_ref=arrived.at[slot],
+            send_sem=f_send.at[d],
+            recv_sem=f_recv.at[d],
+            device_id={"member": other},
+            device_id_type=MESH,
+        )
+
+    def term_copy(slot, via, sem):
+        return pltpu.make_async_remote_copy(
+            src_ref=term.at[slot],
+            dst_ref=term.at[slot],
+            send_sem=t_send.at[sem],
+            recv_sem=t_recv.at[sem],
+            device_id={"member": flip(via)},
+            device_id_type=MESH,
+        )
+
+    def weight_copy(kind, via, shard, own=False, incoming=False):
+        buf = wexp if kind == 0 else wred
+        slot = flip(shard) if incoming else flip(shard ^ via)
+        source = (exp_hbm if kind == 0 else red_hbm) if own else buf.at[slot]
+        return pltpu.make_async_remote_copy(
+            src_ref=source,
+            dst_ref=buf.at[slot],
+            send_sem=w_send.at[shard, kind],
+            recv_sem=w_recv.at[shard, kind],
+            device_id={"member": flip(via)},
+            device_id_type=MESH,
+        )
+
+    top = pl.ds(0, group)
+    bottom = pl.ds(tokens + group, group)
+    first_group = pl.ds(group, group)
+    last_group = pl.ds(tokens, group)
+
+    def halo_up():
+        return pltpu.make_async_remote_copy(
+            src_ref=nx.at[first_group],
+            dst_ref=nx.at[bottom],
+            send_sem=h_send.at[0],
+            recv_sem=h_recv.at[0],
+            device_id={"lat": lat - 1},
+            device_id_type=MESH,
+        )
+
+    def halo_down():
+        return pltpu.make_async_remote_copy(
+            src_ref=nx.at[last_group],
+            dst_ref=nx.at[top],
+            send_sem=h_send.at[1],
+            recv_sem=h_recv.at[1],
+            device_id={"lat": lat + 1},
+            device_id_type=MESH,
+        )
+
+    local["noisy"].start()
+    local["joint"].start()
+    local["frame"].start()
+    barrier = pltpu.get_barrier_semaphore()
+    for d in range(1, 8):
+        pl.semaphore_signal(barrier, inc=1, device_id={"member": flip(d)}, device_id_type=MESH)
+
+    @pl.when(lat > 0)
+    def _():
+        pl.semaphore_signal(barrier, inc=1, device_id={"lat": lat - 1}, device_id_type=MESH)
+
+    @pl.when(lat < lats - 1)
+    def _():
+        pl.semaphore_signal(barrier, inc=1, device_id={"lat": lat + 1}, device_id_type=MESH)
+
+    for name in ("ein", "eout", "qw", "kvw", "ow", "exp", "red"):
+        local[name].start()
+    neighbours = jnp.where(lat > 0, 1, 0) + jnp.where(lat < lats - 1, 1, 0)
+    pl.semaphore_wait(barrier, 7 + neighbours)
+
+    for d in (6, 2, 4, 7, 3, 5, 1):
+        frame_copy(d).start()
+    weight_copy(0, 1, 1, own=True).start()
+    weight_copy(1, 1, 1, own=True).start()
+
+    lane = lax.broadcasted_iota(jnp.int32, (8, 128), 1)
+    padded_table[...] = jnp.zeros_like(padded_table)
+    padded_table[0:heads, 0 : table_ref.shape[1]] = table_ref[...]
+    span = 2 * WIN - 1
+    high = padded_table[...].astype(BF)
+    left_over = padded_table[...] - high.astype(F32)
+    middle = left_over.astype(BF)
+    low = (left_over - middle.astype(F32)).astype(BF)
+    entry = lax.broadcasted_iota(jnp.int32, (256, 128), 0)
+    place = lax.broadcasted_iota(jnp.int32, (256, 128), 1)
+    for col in range(WIN):
+        wanted = (place // WIN) * span + place % WIN - col + WIN - 1
+        hot = jnp.where((entry == wanted) & (place < span * WIN), 1.0, 0.0).astype(BF)
+        row = jnp.dot(high, hot, preferred_element_type=F32)
+        row = row + jnp.dot(middle, hot, preferred_element_type=F32)
+        row = row + jnp.dot(low, hot, preferred_element_type=F32)
+        for head in range(heads):
+            spread[head, col : col + 1, :] = row[head : head + 1, :]
+    for pair in range(heads // 2):
+        for r in range(WIN):
+            first = pltpu.roll(spread[2 * pair], (128 - (WIN - 1 - r) * WIN) % 128, 1)
+            second = pltpu.roll(spread[2 * pair + 1], (64 + 128 - (WIN - 1 - r) * WIN) % 128, 1)
+            bias[pair, r * WIN : (r + 1) * WIN, :] = jnp.where(lane < 64, first, second)
+
+    shift = shift_ref[0]
+    new = lax.broadcasted_iota(jnp.int32, (group, group), 0)
+    old = lax.broadcasted_iota(jnp.int32, (group, group), 1)
+    per_window = group * WIN // cols
+    new_row = (new % per_window) // WIN
+    new_col = (new // per_window) * WIN + new % WIN
+    old_row = old // cols
+    old_col = (old % cols + shift) % cols
+    to_windows = jnp.where((new_row == old_row) & (new_col == old_col), 1.0, 0.0).astype(BF)
+
+    step = 256
+
+    local["noisy"].wait()
+    local["joint"].wait()
+
+    def latents(n, _):
+        at = pl.ds(pl.multiple_of(n * step, step), step)
+        total[:, at] = jnp.dot(noisy[...], joint[0:width, at], preferred_element_type=F32)
+        return 0
+
+    lax.fori_loop(0, width // step, latents, 0)
+
+    local["frame"].wait()
+    local["ein"].wait()
+    local["eout"].wait()
+    for d in range(1, 8):
+        frame_copy(d, incoming=True).wait_recv()
+    local["exp"].wait()
+    local["red"].wait()
+
+    both = jnp.concatenate([arrived[enc_ref[0]], arrived[enc_ref[1]]], axis=0)
+    inner = jax.nn.gelu(jnp.dot(both, ein[...], preferred_element_type=F32)).astype(BF)
+    conditions = jnp.dot(inner, eout[...], preferred_element_type=F32).astype(BF)
+    mine = jnp.dot(conditions[:piece], joint[width : 2 * width, :], preferred_element_type=F32)
+    mine = mine + jnp.dot(conditions[piece:], joint[2 * width :, :], preferred_element_type=F32)
+    term[member] = mine.astype(BF)
+    for d in (6, 2, 4, 1):
+        term_copy(member, d, d).start()
+    weight_copy(0, 2, 2, own=True).start()
+    weight_copy(1, 4, 4, own=True).start()
+    weight_copy(1, 2, 2, own=True).start()
+    weight_copy(0, 4, 4, own=True).start()
+    for d in (2, 4, 6):
+        term_copy(flip(d), d, d).wait_recv()
+        term_copy(flip(d), 1, d + 1).start()
+    term_copy(flip(1), 1, 1).wait_recv()
+    for d in (3, 5, 7):
+        term_copy(flip(d), 1, d).wait_recv()
+
+    for g in (0, 3, 1, 2):
+        at = pl.ds(g * group, group)
+        added = jnp.concatenate([term[2 * g], term[2 * g + 1]], axis=0).astype(F32)
+        natural = (total[at, :] + added).astype(BF)
+        ordered = jnp.dot(to_windows, natural, preferred_element_type=F32)
+        stream[at, :] = ordered.astype(BF)
+        nx[pl.ds((g + 1) * group, group), :] = rms_norm(ordered)
+        if g == 0:
+
+            @pl.when(lat > 0)
+            def _():
+                halo_up().start()
+
+        if g == 3:
+
+            @pl.when(lat < lats - 1)
+            def _():
+                halo_down().start()
+
+    local["qw"].wait()
+    local["kvw"].wait()
+    local["ow"].wait()
+    own = pl.ds(group, tokens)
+
+    def queries(n, _):
+        at = pl.ds(pl.multiple_of(n * step, step), step)
+        q[:, at] = jnp.dot(nx[own, :], qw[:, at], preferred_element_type=F32).astype(BF)
+        return 0
+
+    lax.fori_loop(0, width // step, queries, 0)
+
+    def keyvalues(n, _):
+        at = pl.ds(pl.multiple_of(n * step, step), step)
+        kv[own, at] = jnp.dot(nx[own, :], kvw[:, at], preferred_element_type=F32).astype(BF)
+        return 0
+
+    lax.fori_loop(0, 2 * width // step, keyvalues, 0)
+
+    @pl.when(lat > 0)
+    def _():
+        halo_down().wait_recv()
+
+    @pl.when(lat == 0)
+    def _():
+        nx[top, :] = jnp.zeros((group, width), BF)
+
+    @pl.when(lat < lats - 1)
+    def _():
+        halo_up().wait_recv()
+
+    @pl.when(lat == lats - 1)
+    def _():
+        nx[bottom, :] = jnp.zeros((group, width), BF)
+
+    def halo_keyvalues(n, _):
+        at = pl.ds(pl.multiple_of(n * step, step), step)
+        kv[top, at] = jnp.dot(nx[top, :], kvw[:, at], preferred_element_type=F32).astype(BF)
+        kv[bottom, at] = jnp.dot(nx[bottom, :], kvw[:, at], preferred_element_type=F32).astype(BF)
+        return 0
+
+    lax.fori_loop(0, 2 * width // step, halo_keyvalues, 0)
+
+    weight_copy(0, 2, 2, incoming=True).wait_recv()
+    weight_copy(0, 4, 6).start()
+    weight_copy(0, 1, 3).start()
+    weight_copy(1, 4, 4, incoming=True).wait_recv()
+    weight_copy(1, 2, 6).start()
+    weight_copy(1, 1, 5).start()
+
+    half = per_window
+    lane1 = lax.broadcasted_iota(jnp.int32, (1, 128), 1)
+    left = jnp.where(lane1 < 64, 1.0, 0.0).astype(BF)
+    right = jnp.where(lane1 < 64, 0.0, 1.0).astype(BF)
+
+    def windows(w, _):
+        def rows(g):
+            return pl.ds(pl.multiple_of(g * group + w * half, half), half)
+
+        for band in range(3):
+            groups = {0: (0,), 1: (1, 2), 2: (3,)}[band]
+            for pair in range(heads // 2):
+                lanes = slice(pair * 128, (pair + 1) * 128)
+                vlanes = slice(width + pair * 128, width + (pair + 1) * 128)
+                keys = jnp.concatenate([kv[rows(2 * band), lanes], kv[rows(2 * band + 1), lanes]], axis=0)
+                values = jnp.concatenate([kv[rows(2 * band), vlanes], kv[rows(2 * band + 1), vlanes]], axis=0)
+                keys = jnp.concatenate([keys * left, keys * right], axis=0)
+                values = jnp.concatenate([values * left, values * right], axis=0)
+                asked = [q[rows(g), lanes] for g in groups]
+                asked = asked[0] if len(asked) == 1 else jnp.concatenate(asked, axis=0)
+                scores = lax.dot_general(asked, keys, (((1,), (1,)), ((), ())), preferred_element_type=F32)
+                if band == 0:
+                    near = bias[pair, half : 2 * half, :]
+                elif band == 1:
+                    near = bias[pair]
+                else:
+                    near = bias[pair, 0:half, :]
+                scores = scores * HD ** (-0.5) + near
+                side = lax.broadcasted_iota(jnp.int32, scores.shape, 1)
+                if band == 0:
+                    scores = jnp.where((side % 64 < half) & (lat == 0), -1e30, scores)
+                if band == 2:
+                    scores = jnp.where((side % 64 >= half) & (lat == lats - 1), -1e30, scores)
+                is_left = side < 64
+                high0 = jnp.max(jnp.where(is_left, scores, -3e38), axis=-1, keepdims=True)
+                high1 = jnp.max(jnp.where(is_left, -3e38, scores), axis=-1, keepdims=True)
+                weights = jnp.exp(scores - jnp.where(is_left, high0, high1))
+                sum0 = jnp.sum(jnp.where(is_left, weights, 0.0), axis=-1, keepdims=True)
+                sum1 = jnp.sum(jnp.where(is_left, 0.0, weights), axis=-1, keepdims=True)
+                probs = (weights * jnp.where(is_left, 1.0 / sum0, 1.0 / sum1)).astype(BF)
+                result = jnp.dot(probs, values, preferred_element_type=F32).astype(BF)
+                for i, g in enumerate(groups):
+                    mixed[rows(g), lanes] = result[i * half : (i + 1) * half]
+        return 0
+
+    lax.fori_loop(0, cols // WIN, windows, 0)
+
+    weight_copy(1, 2, 2, incoming=True).wait_recv()
+    weight_copy(1, 1, 3).start()
+    weight_copy(0, 4, 4, incoming=True).wait_recv()
+    weight_copy(0, 1, 5).start()
+
+    def project(n, _):
+        at = pl.ds(pl.multiple_of(n * step, step), step)
+        total[:, at] = stream[:, at].astype(F32) + jnp.dot(mixed[...], ow[:, at], preferred_element_type=F32)
+        return 0
+
+    lax.fori_loop(0, width // step, project, 0)
+    @pl.when(lat > 0)
+    def _():
+        halo_up().wait_send()
+
+    @pl.when(lat < lats - 1)
+    def _():
+        halo_down().wait_send()
+
+    for g in range(4):
+        at = pl.ds(g * group, group)
+        attended = total[at, :].astype(BF).astype(F32)
+        total[at, :] = attended
+        q[at, :] = rms_norm(attended)
+
+    def feed(chip):
+        for s in range(2):
+            slot = chip * 2 + s
+            hidden = jax.nn.gelu(
+                lax.dot_general(q[...], wexp[slot], (((1,), (1,)), ((), ())), preferred_element_type=F32)
+            ).astype(BF)
+            mixed[:, 0:part] = hidden
+
+            def reduce(n, _):
+                at = pl.ds(pl.multiple_of(n * step, step), step)
+                total[:, at] += jnp.dot(mixed[:, 0:part], wred[slot, :, at], preferred_element_type=F32)
+                return 0
+
+            lax.fori_loop(0, width // step, reduce, 0)
+
+    chip = member // 2
+
+    def other_chip(d):
+        return flip(d) // 2
+
+    for kind in range(2):
+        weight_copy(kind, 1, 1, incoming=True).wait_recv()
+    feed(chip)
+    weight_copy(0, 4, 6, incoming=True).wait_recv()
+    weight_copy(0, 1, 7).start()
+    weight_copy(1, 2, 6, incoming=True).wait_recv()
+    weight_copy(1, 1, 7).start()
+    for kind in range(2):
+        weight_copy(kind, 1, 3, incoming=True).wait_recv()
+    feed(other_chip(2))
+    for kind in range(2):
+        weight_copy(kind, 1, 5, incoming=True).wait_recv()
+    feed(other_chip(4))
+    for kind in range(2):
+        weight_copy(kind, 1, 7, incoming=True).wait_recv()
+    feed(other_chip(6))
+
+    for g in range(4):
+        at = pl.ds(g * group, group)
+        natural = lax.dot_general(
+            to_windows, total[at, :].astype(BF), (((0,), (0,)), ((), ())), preferred_element_type=F32
+        )
+        out_ref[at, :] = natural.astype(BF)
+
+    for d in range(1, 8):
+        frame_copy(d).wait_send()
+        term_copy(member, d if d in (1, 2, 4, 6) else 1, d).wait_send()
+        for kind in range(2):
+            weight_copy(kind, 1, d).wait_send()
+
+
+def fused(
+    noisy_latents,
+    frames,
+    encoder_members,
+    window_shift,
+    encoder_in,
+    encoder_out,
+    joint_weight,
+    query_weight,
+    keyvalue_weight,
+    output_weight,
+    position_bias,
+    expand_weight,
+    reduce_weight,
+):
+    width = noisy_latents.shape[-1]
+    tokens = noisy_latents.shape[1] * noisy_latents.shape[2]
+    part = expand_weight.shape[0]
+    heads = position_bias.shape[0]
+    group = tokens // 4
+    smem = pl.BlockSpec(memory_space=pltpu.SMEM)
+    vmem = pl.BlockSpec(memory_space=pltpu.VMEM)
+    anywhere = pl.BlockSpec(memory_space=pl.ANY)
+    dma = pltpu.SemaphoreType.DMA
+    out = pl.pallas_call(
+        fused_kernel,
+        out_shape=jax.ShapeDtypeStruct((tokens, width), BF),
+        in_specs=[smem, smem] + [anywhere] * 8 + [vmem] + [anywhere] * 2,
+        out_specs=vmem,
+        scratch_shapes=[
+            pltpu.VMEM((tokens, width), BF),
+            pltpu.VMEM((width, width), BF),
+            pltpu.VMEM((width, width), BF),
+            pltpu.VMEM((3 * width, width), BF),
+            pltpu.VMEM((width, width), BF),
+            pltpu.VMEM((width, 2 * width), BF),
+            pltpu.VMEM((width, width), BF),
+            pltpu.VMEM((8, part, width), BF),
+            pltpu.VMEM((8, part, width), BF),
+            pltpu.VMEM((8, tokens // 8, width), BF),
+            pltpu.VMEM((8, tokens // 8, width), BF),
+            pltpu.VMEM((tokens, width), F32),
+            pltpu.VMEM((tokens, width), BF),
+            pltpu.VMEM((tokens + 2 * group, width), BF),
+            pltpu.VMEM((tokens, width), BF),
+            pltpu.VMEM((tokens + 2 * group, 2 * width), BF),
+            pltpu.VMEM((tokens, width), BF),
+            pltpu.VMEM((heads // 2, WIN * WIN, 128), F32),
+            pltpu.VMEM((16, 256), F32),
+            pltpu.VMEM((heads, WIN, 128), F32),
+            dma((10,)),
+            dma((8,)),
+            dma((8,)),
+            dma((8,)),
+            dma((8,)),
+            dma((8, 2)),
+            dma((8, 2)),
+            dma((2,)),
+            dma((2,)),
+        ],
+        compiler_params=pltpu.CompilerParams(
+            collective_id=0, has_side_effects=True, vmem_limit_bytes=56 * 1024 * 1024
+        ),
+    )(
+        encoder_members,
+        window_shift,
+        noisy_latents.reshape(tokens, width),
+        frames.reshape(tokens, width),
+        encoder_in,
+        encoder_out,
+        joint_weight,
+        query_weight,
+        keyvalue_weight,
+        output_weight,
+        position_bias,
+        expand_weight,
+        reduce_weight,
+    )
+    return out.reshape(noisy_latents.shape)
+
+
 def solution(mesh):
+    body = fused if mesh.shape["member"] == 8 else per_device
     return jax.shard_map(
-        per_device,
+        body,
         mesh=mesh,
         in_specs=(
             P("member", "lat", None, None),

time: 172 us -> 78.8 us (0.46)
  Pallas kernels: 0 us -> 75.8 us
  waiting for transfers between devices: 55 us -> 0 us
  matrix products: 43.3 us -> 0 us
  local copies, waits for them, and re-layouts: 43.2 us -> 2.06 us
  between operations: 15.2 us -> 0.66 us
  other arithmetic: 9.32 us -> 0 us
  starting transfers between devices: 5.74 us -> 0 us
    pallas_call x0 -> x1, Pallas kernels: none -> 75.8 us  [fused(): pl.pallas_call(fused_kernel, out_shape=jax.ShapeDtypeStruct((tokens, widt...]
    psum x1 -> x0, waiting for transfers between devices: 39.3 us -> none  [broadcast(): return lax.psum(jnp.where(mine, array, jnp.zeros_like(array)), axis)]
    dot_general x10 -> x0, matrix products: 36 us -> none  [the longest x1 10.4 us: per_device(): jnp.dot(hidden, lax.all_gather(reduce_weight, 'member', axis=0, tiled=Tru...]
    gather x2 -> x0, local copies, waits for them, and re-layouts: 16.9 us -> none  [window_attention(): bias = position_bias[:, offset_table(WIN)]]
    reshape x5 -> x0, local copies, waits for them, and re-layouts: 16 us -> none  [the longest x3 10.2 us: arrange(): block = block.reshape(row_groups, WIN, col_groups, WIN, heads, HD)]
    all_gather x2 -> x0, waiting for transfers between devices: 12.2 us -> none  [the longest x1 12.2 us: per_device(): lax.all_gather(reduce_weight, 'member', axis=0, tiled=True)]
    sub x1 -> x0, matrix products: 7.33 us -> none  [window_attention(): weights = jnp.exp(scores - highest)]
    concatenate x3 -> x0, other arithmetic: 6.75 us -> none  [the longest x2 5.35 us: arrange(): block = jnp.roll(block, shift, axis=1)]
  transfers between devices with their start and end apart: 5 -> 0, of which waited for: 3 -> 0; matrix products, arithmetic and copies ran while one was open for 47% -> 0% of each run, Pallas kernels for 0% -> 0%
where the time goes in v1:
time: 78.8 us; the launch traced here: 78.5 us
  Pallas kernels  75.8 us (96%)
  local copies, waits for them, and re-layouts  2.06 us (3%)
    pallas_call x1, Pallas kernels, fused(): pl.pallas_call(fused_kernel, out_shape=jax.ShapeDtypeStruct((tokens, widt...  75.8 us
    unnamed x1, local copies, waits for them, and re-layouts  2.06 us

profile of v1, /device:TPU:0, one launch (start us, length us, event | category | flops | bytes accessed | tf_op | source)
XLA Modules:
  0.0 78.5 jit_solution(13869236711446063427)
XLA Ops:
  0.7 75.8 %shard_map.127 = bf16[512,768]{1,0:T(8,128)(2,1)} custom-call(s32[2]{0:T(128)} %enc_ref.1, s32[1]{0:T(128)S(6)} %copy.15.shift_ref, bf16[512,768]{1,0:T(8,128)(2,1)} %bitcast.4, bf16[512,768]{1,0:T(8,128)(2,1)} %bitcast.5, bf16[768,768]{1,0:T(8,128)(2,1)} %ein_hbm.1, bf16[768,768]{1,0:T(8,128)(2,1)} %eout_hbm.1, bf16[2304,768]{1,0:T(8,128)(2,1)} %joint_hbm.1, ...), custom_call_target="tpu_custom_call" | custom-call | tf_op jit(solution)/shard_map/pallas_call | solution.py:624
  76.4 2.1 %copy.16 = bf16[1,16,32,768]{3,2,1,0:T(8,128)(2,1)} copy(bf16[1,16,32,768]{3,2,1,0:T(8,128)(2,1)} %bitcast.3) | data formatting | bytes 1572864

commit v2 on v1

--- a/solution.py
+++ b/solution.py
@@ -223,13 +223,16 @@
     tokens, width = noisy.shape
     piece = tokens // 8
     group = tokens // 4
-    part = wexp.shape[1]
+    part = wexp.shape[1] // 2
     cols = group // (WIN // 2)
     heads = table_ref.shape[0]
     y, x, c = member // 4, (member // 2) % 2, member % 2
 
     def flip(d):
         return ((y + d // 4) % 2) * 4 + ((x + (d // 2) % 2) % 2) * 2 + (c + d % 2) % 2
+
+    def shard(buf, slot):
+        return buf.at[slot // 2, pl.ds((slot % 2) * part, part)]
 
     local = {}
     todo = [
@@ -240,8 +243,8 @@
         ("qw", qw_hbm, qw),
         ("kvw", kvw_hbm, kvw),
         ("ow", ow_hbm, ow),
-        ("exp", exp_hbm, wexp.at[member]),
-        ("red", red_hbm, wred.at[member]),
+        ("exp", exp_hbm, shard(wexp, member)),
+        ("red", red_hbm, shard(wred, member)),
         ("frame", frames_hbm.at[pl.ds(member * piece, piece)], arrived.at[member]),
     ]
     for i, (name, source, target) in enumerate(todo):
@@ -269,15 +272,15 @@
             device_id_type=MESH,
         )
 
-    def weight_copy(kind, via, shard, own=False, incoming=False):
+    def weight_copy(kind, via, origin, own=False, incoming=False):
         buf = wexp if kind == 0 else wred
-        slot = flip(shard) if incoming else flip(shard ^ via)
-        source = (exp_hbm if kind == 0 else red_hbm) if own else buf.at[slot]
+        slot = flip(origin) if incoming else flip(origin ^ via)
+        source = (exp_hbm if kind == 0 else red_hbm) if own else shard(buf, slot)
         return pltpu.make_async_remote_copy(
             src_ref=source,
-            dst_ref=buf.at[slot],
-            send_sem=w_send.at[shard, kind],
-            recv_sem=w_recv.at[shard, kind],
+            dst_ref=shard(buf, slot),
+            send_sem=w_send.at[origin, kind],
+            recv_sem=w_recv.at[origin, kind],
             device_id={"member": flip(via)},
             device_id_type=MESH,
         )
@@ -329,6 +332,8 @@
 
     for d in (6, 2, 4, 7, 3, 5, 1):
         frame_copy(d).start()
+    weight_copy(0, 2, 2, own=True).start()
+    weight_copy(1, 4, 4, own=True).start()
     weight_copy(0, 1, 1, own=True).start()
     weight_copy(1, 1, 1, own=True).start()
 
@@ -394,8 +399,6 @@
     term[member] = mine.astype(BF)
     for d in (6, 2, 4, 1):
         term_copy(member, d, d).start()
-    weight_copy(0, 2, 2, own=True).start()
-    weight_copy(1, 4, 4, own=True).start()
     weight_copy(1, 2, 2, own=True).start()
     weight_copy(0, 4, 4, own=True).start()
     for d in (2, 4, 6):
@@ -479,20 +482,26 @@
     left = jnp.where(lane1 < 64, 1.0, 0.0).astype(BF)
     right = jnp.where(lane1 < 64, 0.0, 1.0).astype(BF)
 
+    is_left = lane1 < 64
+    north = (lane1 % 64 < half) & (lat == 0)
+    south = (lane1 % 64 >= half) & (lat == lats - 1)
+    from_left = lax.broadcasted_iota(jnp.int32, (128, 128), 0) < 64
+    to_left = lax.broadcasted_iota(jnp.int32, (128, 128), 1) < 64
+    ones = jnp.where(from_left == to_left, 1.0, 0.0).astype(BF)
+    owned = {0: (0,), 1: (1, 2), 2: (3,)}
+
     def windows(w, _):
         def rows(g):
             return pl.ds(pl.multiple_of(g * group + w * half, half), half)
 
-        for band in range(3):
-            groups = {0: (0,), 1: (1, 2), 2: (3,)}[band]
-            for pair in range(heads // 2):
+        for bands in ((1,), (0, 2)):
+            jobs = [(band, pair) for band in bands for pair in range(heads // 2)]
+            scored = []
+            for band, pair in jobs:
                 lanes = slice(pair * 128, (pair + 1) * 128)
-                vlanes = slice(width + pair * 128, width + (pair + 1) * 128)
                 keys = jnp.concatenate([kv[rows(2 * band), lanes], kv[rows(2 * band + 1), lanes]], axis=0)
-                values = jnp.concatenate([kv[rows(2 * band), vlanes], kv[rows(2 * band + 1), vlanes]], axis=0)
                 keys = jnp.concatenate([keys * left, keys * right], axis=0)
-                values = jnp.concatenate([values * left, values * right], axis=0)
-                asked = [q[rows(g), lanes] for g in groups]
+                asked = [q[rows(g), lanes] for g in owned[band]]
                 asked = asked[0] if len(asked) == 1 else jnp.concatenate(asked, axis=0)
                 scores = lax.dot_general(asked, keys, (((1,), (1,)), ((), ())), preferred_element_type=F32)
                 if band == 0:
@@ -502,20 +511,25 @@
                 else:
                     near = bias[pair, 0:half, :]
                 scores = scores * HD ** (-0.5) + near
-                side = lax.broadcasted_iota(jnp.int32, scores.shape, 1)
                 if band == 0:
-                    scores = jnp.where((side % 64 < half) & (lat == 0), -1e30, scores)
+                    scores = jnp.where(north, -1e30, scores)
                 if band == 2:
-                    scores = jnp.where((side % 64 >= half) & (lat == lats - 1), -1e30, scores)
-                is_left = side < 64
+                    scores = jnp.where(south, -1e30, scores)
+                scored.append(scores)
+            weighed = []
+            for scores in scored:
                 high0 = jnp.max(jnp.where(is_left, scores, -3e38), axis=-1, keepdims=True)
                 high1 = jnp.max(jnp.where(is_left, -3e38, scores), axis=-1, keepdims=True)
-                weights = jnp.exp(scores - jnp.where(is_left, high0, high1))
-                sum0 = jnp.sum(jnp.where(is_left, weights, 0.0), axis=-1, keepdims=True)
-                sum1 = jnp.sum(jnp.where(is_left, 0.0, weights), axis=-1, keepdims=True)
-                probs = (weights * jnp.where(is_left, 1.0 / sum0, 1.0 / sum1)).astype(BF)
-                result = jnp.dot(probs, values, preferred_element_type=F32).astype(BF)
-                for i, g in enumerate(groups):
+                weighed.append(jnp.exp(scores - jnp.where(is_left, high0, high1)).astype(BF))
+            for (band, pair), weights in zip(jobs, weighed):
+                lanes = slice(pair * 128, (pair + 1) * 128)
+                vlanes = slice(width + pair * 128, width + (pair + 1) * 128)
+                values = jnp.concatenate([kv[rows(2 * band), vlanes], kv[rows(2 * band + 1), vlanes]], axis=0)
+                values = jnp.concatenate([values * left, values * right], axis=0)
+                values = jnp.concatenate([values, ones], axis=1)
+                result = jnp.dot(weights, values, preferred_element_type=F32)
+                result = (result[:, :128] / result[:, 128:]).astype(BF)
+                for i, g in enumerate(owned[band]):
                     mixed[rows(g), lanes] = result[i * half : (i + 1) * half]
         return 0
 
@@ -547,19 +561,23 @@
         q[at, :] = rms_norm(attended)
 
     def feed(chip):
-        for s in range(2):
-            slot = chip * 2 + s
-            hidden = jax.nn.gelu(
-                lax.dot_general(q[...], wexp[slot], (((1,), (1,)), ((), ())), preferred_element_type=F32)
+        def expand(n, _):
+            at = pl.ds(pl.multiple_of(n * step, step), step)
+            mixed[:, at] = jax.nn.gelu(
+                lax.dot_general(
+                    q[...], wexp[chip, at, :], (((1,), (1,)), ((), ())), preferred_element_type=F32
+                )
             ).astype(BF)
-            mixed[:, 0:part] = hidden
-
-            def reduce(n, _):
-                at = pl.ds(pl.multiple_of(n * step, step), step)
-                total[:, at] += jnp.dot(mixed[:, 0:part], wred[slot, :, at], preferred_element_type=F32)
-                return 0
-
-            lax.fori_loop(0, width // step, reduce, 0)
+            return 0
+
+        lax.fori_loop(0, 2 * part // step, expand, 0)
+
+        def reduce(n, _):
+            at = pl.ds(pl.multiple_of(n * step, step), step)
+            total[:, at] += jnp.dot(mixed[...], wred[chip, :, at], preferred_element_type=F32)
+            return 0
+
+        lax.fori_loop(0, width // step, reduce, 0)
 
     chip = member // 2
 
@@ -634,8 +652,8 @@
             pltpu.VMEM((width, width), BF),
             pltpu.VMEM((width, 2 * width), BF),
             pltpu.VMEM((width, width), BF),
-            pltpu.VMEM((8, part, width), BF),
-            pltpu.VMEM((8, part, width), BF),
+            pltpu.VMEM((4, 2 * part, width), BF),
+            pltpu.VMEM((4, 2 * part, width), BF),
             pltpu.VMEM((8, tokens // 8, width), BF),
             pltpu.VMEM((8, tokens // 8, width), BF),
             pltpu.VMEM((tokens, width), F32),

time: 78.8 us -> 69.6 us (0.88)
  Pallas kernels: 75.8 us -> 66.7 us
    pallas_call x1, Pallas kernels: 75.8 us -> 66.7 us  [fused(): pl.pallas_call(fused_kernel, out_shape=jax.ShapeDtypeStruct((tokens, widt...]
where the time goes in v2:
time: 69.6 us; the launch traced here: 69.4 us
  Pallas kernels  66.7 us (96%)
  local copies, waits for them, and re-layouts  2.06 us (3%)
    pallas_call x1, Pallas kernels, fused(): pl.pallas_call(fused_kernel, out_shape=jax.ShapeDtypeStruct((tokens, widt...  66.7 us
    unnamed x1, local copies, waits for them, and re-layouts  2.06 us

profile of v2, /device:TPU:0, one launch (start us, length us, event | category | flops | bytes accessed | tf_op | source)
XLA Modules:
  0.0 69.4 jit_solution(6431844576148125498)
XLA Ops:
  0.7 66.7 %shard_map.127 = bf16[512,768]{1,0:T(8,128)(2,1)} custom-call(s32[2]{0:T(128)} %enc_ref.1, s32[1]{0:T(128)S(6)} %copy.15.shift_ref, bf16[512,768]{1,0:T(8,128)(2,1)} %bitcast.4, bf16[512,768]{1,0:T(8,128)(2,1)} %bitcast.5, bf16[768,768]{1,0:T(8,128)(2,1)} %ein_hbm.1, bf16[768,768]{1,0:T(8,128)(2,1)} %eout_hbm.1, bf16[2304,768]{1,0:T(8,128)(2,1)} %joint_hbm.1, ...), custom_call_target="tpu_custom_call" | custom-call | tf_op jit(solution)/shard_map/pallas_call | solution.py:642
  67.3 2.1 %copy.16 = bf16[1,16,32,768]{3,2,1,0:T(8,128)(2,1)} copy(bf16[1,16,32,768]{3,2,1,0:T(8,128)(2,1)} %bitcast.3) | data formatting | bytes 1572864
